TPU v7x, 256 devices: a whole 4x4x8 slice. The times are simulated.
256 devices in a mesh: row: 16 (over y, z_lo, core), col: 16 (over x, z_hi).
Axes of the slice: x: 4, y: 4, z: 8 (z_hi: 4, z_lo: 2; z = z_hi * 2 + z_lo), core: 2. Of those that a mesh axis runs over, the one named last changes fastest.
Arguments:
- coeffs: float32 [8192, 8192], P('row', 'col'), may hold values from -8 to 8, as said below
- features: float32 [8192, 512], P('row'), may hold values from -0.6 to 0.6
- factors: float32 [8192, 256], P('row'), may hold values from -1.8 to 1.8
Outputs:
- grad_coeffs: float32 [8192, 8192], P('row', 'col')
- grad_features: float32 [8192, 512], P('row', 'col')
Inputs may be any that keep to these rules, and one draw needn't show every extreme that they name: `coeffs`: real coefficients.
All inputs are finite; a program needn't handle non-finite values.
Results may differ from a plain program's by a relative error of at most 0.0003.
Values sent between devices are 32-bit elements; how exact they have to be, the bound alone decides.
A program may use at most 64 MiB of HBM per device.

v0:
```python
import jax
import jax.numpy as jnp
from jax import lax
from jax.sharding import PartitionSpec as P


def from_root(value, axis, root):
    mine = lax.axis_index(axis) == root
    return lax.psum(jnp.where(mine, value, jnp.zeros_like(value)), axis)


def contract_last(left, right):
    return lax.dot_general(
        left,
        right,
        (((1,), (1,)), ((), ())),
        precision=lax.Precision.HIGHEST,
        preferred_element_type=jnp.float32,
    )


def per_device(coeffs, features, factors):
    highest = lax.Precision.HIGHEST
    row_count = lax.axis_size("row")
    col_count = lax.axis_size("col")
    fold_ratio = col_count // row_count
    own_rows, own_cols = coeffs.shape
    col_index = lax.axis_index("col")
    root_row = col_index // fold_ratio
    block_features, block_factors = (
        from_root(features, "row", root_row),
        from_root(factors, "row", root_row),
    )
    partial_sum = jnp.dot(
        coeffs, block_features, precision=highest, preferred_element_type=jnp.float32
    )
    share_width = features.shape[1] // col_count
    residual = lax.psum(partial_sum, "col") - features
    piece_rows = own_cols // row_count
    moved = lax.all_to_all(
        lax.all_to_all(coeffs.T, "row", split_axis=0, concat_axis=1, tiled=True),
        "col",
        split_axis=1,
        concat_axis=0,
        tiled=True,
    )
    moved = lax.all_to_all(moved, "row", split_axis=0, concat_axis=0, tiled=True)
    mirrored = (
        moved.reshape(row_count, fold_ratio, piece_rows, own_cols)
        .transpose(1, 0, 2, 3)
        .reshape(own_rows, own_cols)
    )
    symmetric = 0.5 * (coeffs * coeffs + mirrored * mirrored)
    relation = symmetric - contract_last(factors, block_factors)
    grad_coeffs = contract_last(residual, block_features) + 2.0 * coeffs * relation
    residual_share = lax.dynamic_slice_in_dim(residual, col_index * share_width, share_width, 1)
    block_residual = from_root(residual, "row", root_row)
    terms = jnp.dot(mirrored, block_residual, precision=highest, preferred_element_type=jnp.float32)
    gathered = lax.psum_scatter(terms, "col", scatter_dimension=1, tiled=True)
    grad_features = gathered - residual_share
    return (grad_coeffs, grad_features)


def solution(mesh):
    in_specs = (P("row", "col"), P("row", None), P("row", None))
    out_specs = (P("row", "col"), P("row", "col"))
    return jax.shard_map(
        per_device, mesh=mesh, in_specs=in_specs, out_specs=out_specs, check_vma=False
    )
```

profile of v0, /device:TPU:5, one launch (start us, length us, event | category | flops | bytes accessed | tf_op | source)
XLA Modules:
  0.0 555.5 jit_solution(11611411427292832615)
XLA Ops:
  7.2 2.6 copy.11
  9.7 0.0 copy-start.5
  9.7 6.6 %all-to-all-start = ((f32[16,32,512]{2,1,0:T(8,128)}), f32[16,32,512]{2,1,0:T(8,128)S(1)}, u32[]{:S(2)}, u32[]{:S(2)}) async-start(f32[16,32,512]{2,1,0:T(8,128)} %bitcast.2), calls=%async_computation | async-start | bytes 2097152 | tf_op jit(solution)/shard_map/all_to_all | solution.py:41
  16.4 0.0 all-reduce.5.cloned.1.call-start
  16.4 0.0 copy-done.5
  16.4 0.3 copy.9
  16.8 1.1 broadcast_select_fusion.1
  17.8 0.0 all-reduce.5.cloned.1.call-update
  17.8 14.3 %all-to-all-done = f32[16,32,512]{2,1,0:T(8,128)S(1)} async-done(((f32[16,32,512]{2,1,0:T(8,128)}), f32[16,32,512]{2,1,0:T(8,128)S(1)}, u32[]{:S(2)}, u32[]{:S(2)}) %all-to-all-start) | async-done | bytes 1048608 | tf_op jit(solution)/shard_map/all_to_all | solution.py:41
  32.2 0.0 copy-start.3
  32.2 1.0 copy-done.3
  33.2 0.0 copy-start
  33.2 10.1 %all-to-all-start.1 = ((f32[32,16,512]{2,0,1:T(8,128)}), f32[32,16,512]{2,0,1:T(8,128)S(1)}, u32[]{:S(2)}, u32[]{:S(2)}) async-start(f32[32,16,512]{2,0,1:T(8,128)} %bitcast.29), calls=%async_computation.1 | async-start | bytes 2097152 | tf_op jit(solution)/shard_map/all_to_all | solution.py:40
  43.3 0.0 all-reduce.7.cloned.1.call-start
  43.3 113.7 %all-reduce.5.cloned.1.call-done = f32[512,512]{0,1:T(8,128)} async-done(((f32[512,512]{0,1:T(8,128)}), f32[512,512]{0,1:T(8,128)}) %all-reduce.5.cloned.1.call-update) | async-done | bytes 1048592 | tf_op jit(solution)/shard_map/psum | solution.py:9
  157.1 0.0 copy-done
  157.1 4.1 convolution_bitcast_fusion.2
  161.1 0.0 all-reduce.7.cloned.1.call-update
  161.2 0.0 all-to-all-done.1
  161.2 0.0 copy-start.2
  161.2 1.0 copy-done.2
  162.1 5.8 %all-to-all-start.2 = ((f32[16,32,512]{2,1,0:T(8,128)}), f32[16,32,512]{2,1,0:T(8,128)S(1)}, u32[]{:S(2)}, u32[]{:S(2)}) async-start(f32[16,32,512]{2,1,0:T(8,128)} %bitcast.28), calls=%async_computation.2 | async-start | bytes 2097152 | tf_op jit(solution)/shard_map/all_to_all | solution.py:47
  167.9 0.0 all-reduce.9.cloned.1.call-start
  168.0 0.8 broadcast_select_fusion.2
  168.8 148.0 %all-reduce.7.cloned.1.call-done = f32[512,512]{0,1:T(8,128)} async-done(((f32[512,512]{0,1:T(8,128)}), f32[512,512]{0,1:T(8,128)}) %all-reduce.7.cloned.1.call-update) | async-done | bytes 1048592 | tf_op jit(solution)/shard_map/psum | solution.py:38
  316.9 2.8 broadcast_select_fusion
  319.7 0.0 all-reduce.9.cloned.1.call-update
  319.7 0.0 reduce-scatter.2.cloned.1.call-start
  319.8 139.5 %all-reduce.9.cloned.1.call-done = (f32[512,256]{1,0:T(8,128)}, f32[512,512]{0,1:T(8,128)}) async-done(((f32[512,256]{1,0:T(8,128)}, f32[512,512]{0,1:T(8,128)}), (f32[512,256]{1,0:T(8,128)}, f32[512,512]{0,1:T(8,128)})) %all-reduce.9.cloned.1.call-update) | async-done | bytes 1572880 | tf_op jit(solution)/shard_map/psum | solution.py:9
  459.3 0.0 all-to-all-done.2
  459.3 4.1 convolution_bitcast_fusion
  463.3 0.0 copy-start.1
  463.3 0.0 reduce-scatter.2.cloned.1.call-update
  463.4 1.2 copy-done.1
  464.6 0.0 copy-start.4
  464.6 0.0 copy-start.6
  464.6 3.2 fusion.3
  467.7 0.0 copy-done.4
  467.7 0.0 copy-done.6
  467.7 2.2 fusion.2
  470.0 77.5 %reduce-scatter.2.cloned.1.call-done = f32[512,32]{0,1:T(8,128)} async-done(((f32[512,512]{0,1:T(8,128)}), f32[512,32]{0,1:T(8,128)}) %reduce-scatter.2.cloned.1.call-update) | async-done | bytes 65552 | tf_op jit(solution)/shard_map/reduce_scatter | solution.py:59
  547.5 1.5 dynamic-slice_subtract_fusion
Async XLA Ops:
  9.7 6.7 %copy-start.5 = (f32[512,512]{1,0:T(8,128)S(1)}, f32[512,512]{1,0:T(8,128)}, u32[]{:S(2)}) copy-start(f32[512,512]{1,0:T(8,128)} %param.4) | copy-start | bytes 3145732
  9.7 22.5 %all-to-all-start = ((f32[16,32,512]{2,1,0:T(8,128)}), f32[16,32,512]{2,1,0:T(8,128)S(1)}, u32[]{:S(2)}, u32[]{:S(2)}) async-start(f32[16,32,512]{2,1,0:T(8,128)} %bitcast.2), calls=%async_computation | async-start | bytes 2097152 | tf_op jit(solution)/shard_map/all_to_all | solution.py:41
  16.4 140.7 %all-reduce.5.cloned.1.call-start = ((), (), s32[]{:S(2)}) async-start(), calls=%async_computation.4 | async-start | bytes 2097152 | tf_op jit(solution)/shard_map/psum | solution.py:9
  32.2 1.0 copy-start.3
  33.2 123.9 %copy-start = (f32[512,512]{1,0:T(8,128)S(1)}, f32[512,512]{1,0:T(8,128)}, u32[]{:S(2)}) copy-start(f32[512,512]{1,0:T(8,128)} %param.3) | copy-start | bytes 3145732
  33.2 128.0 %all-to-all-start.1 = ((f32[32,16,512]{2,0,1:T(8,128)}), f32[32,16,512]{2,0,1:T(8,128)S(1)}, u32[]{:S(2)}, u32[]{:S(2)}) async-start(f32[32,16,512]{2,0,1:T(8,128)} %bitcast.29), calls=%async_computation.1 | async-start | bytes 2097152 | tf_op jit(solution)/shard_map/all_to_all | solution.py:40
  43.3 273.6 %all-reduce.7.cloned.1.call-start = ((), (), s32[]{:S(2)}) async-start(), calls=%async_computation.5 | async-start | bytes 2097152 | tf_op jit(solution)/shard_map/psum | solution.py:38
  161.2 1.0 copy-start.2
  162.1 297.1 %all-to-all-start.2 = ((f32[16,32,512]{2,1,0:T(8,128)}), f32[16,32,512]{2,1,0:T(8,128)S(1)}, u32[]{:S(2)}, u32[]{:S(2)}) async-start(f32[16,32,512]{2,1,0:T(8,128)} %bitcast.28), calls=%async_computation.2 | async-start | bytes 2097152 | tf_op jit(solution)/shard_map/all_to_all | solution.py:47
  167.9 291.3 %all-reduce.9.cloned.1.call-start = ((), (), s32[]{:S(2)}) async-start(), calls=%async_computation.7 | async-start | bytes 3145728 | tf_op jit(solution)/shard_map/psum | solution.py:9
  319.7 227.8 %reduce-scatter.2.cloned.1.call-start = ((), (), s32[]{:S(2)}) async-start(), calls=%async_computation.6 | async-start | bytes 1114112 | tf_op jit(solution)/shard_map/reduce_scatter | solution.py:59
  463.3 1.2 copy-start.1
  464.6 3.2 copy-start.4
  464.6 3.2 copy-start.6
Sparse Core Ops, SparseCore 0:
  20.4 136.6 all-reduce.4
  161.3 155.5 all-reduce.6
  320.1 139.0 all-reduce.8
  463.5 83.9 reduce-scatter.1
where the time goes:
time: 559 us; the launch traced here: 555 us
  waiting for transfers between devices  493 us (88%)
  starting transfers between devices  22.7 us (4%)
  between operations  13.8 us (2%)
  matrix products  13.5 us (2%)
  other arithmetic  6.22 us (1%)
  local copies, waits for them, and re-layouts  6.04 us (1%)
    psum x2, waiting for transfers between devices, from_root(): return lax.psum(jnp.where(mine, value, jnp.zeros_like(value)), axis)  253 us
    psum x1, waiting for transfers between devices, per_device(): residual = lax.psum(partial_sum, 'col') - features  148 us
    reduce_scatter x1, waiting for transfers between devices, per_device(): gathered = lax.psum_scatter(terms, 'col', scatter_dimension=1, tiled=True)  77.5 us
    all_to_all x1, waiting for transfers between devices, per_device(): lax.all_to_all(coeffs.T, 'row', split_axis=0, concat_axis=1, tiled=True)  14.3 us
  transfers between devices with their start and end apart: 7, of which 5 were waited for; matrix products, arithmetic and copies ran while one was open for 3% of the time, Pallas kernels for 0%

commit v1 on v0

v1 whole, which is shorter than its diff:
```python
import functools

import jax
import jax.numpy as jnp
from jax import lax
from jax.experimental import pallas as pl
from jax.experimental.pallas import tpu as pltpu
from jax.sharding import PartitionSpec as P

F32, BF16 = jnp.float32, jnp.bfloat16
MESH = pl.DeviceIdType.MESH
NN = (((1,), (0,)), ((), ()))
NT = (((1,), (1,)), ((), ()))
S = 32
G = 128


def split(a):
    hi = a.astype(BF16)
    return hi, (a - hi.astype(F32)).astype(BF16)


def dot3(a, b, dims):
    ah, al = a
    bh, bl = b
    dot = functools.partial(lax.dot_general, dimension_numbers=dims, preferred_element_type=F32)
    return dot(ah, bh) + (dot(ah, bl) + dot(al, bh))


def kernel(
    c_ref, z_ref, h_ref, dc_ref, dz_ref,
    zslab, zct, hc, m, ch, cl, pt, ra, sb, rb, rt, tt, rc, se, rd, tot, dzt,
    send, rsend,
    st_sem, m_sem, zg_sem, zc_sem, hg_sem, hcs_sem, ra_sem, rb_sem, ag_sem, rc_sem, rd_sem, fin_sem,
):
    r, c = lax.axis_index("row"), lax.axis_index("col")
    y, zl, co = r // 4, (r // 2) % 2, r % 2
    x, zh = c // 4, c % 4
    swap = r != c
    mate = r + 1 - 2 * co

    def rows(start, size=S):
        return pl.ds(pl.multiple_of(start * S, S), size)

    def row_peer(dy, dz):
        return ((y + dy) % 4) * 4 + ((zl + dz) % 2) * 2 + co

    def row_from(dy, dz):
        return ((y - dy) % 4) * 4 + ((zl - dz) % 2) * 2 + co

    count = [0]
    pending = []

    def copy(src, dst, sem, row, col):
        n = count[0]
        count[0] += 1
        return pltpu.make_async_remote_copy(
            src_ref=src, dst_ref=dst, send_sem=send.at[n], recv_sem=sem,
            device_id={"row": row, "col": col}, device_id_type=MESH,
        )

    def put(src, dst, sem, row, col):
        one = copy(src, dst, sem, row, col)
        one.start()
        pending.append(one)

    def got(dst, sem):
        pltpu.make_async_remote_copy(
            src_ref=dst, dst_ref=dst, send_sem=rsend, recv_sem=sem,
            device_id={"row": mate, "col": c}, device_id_type=MESH,
        ).wait_recv()

    offsets = [(dy, dz) for dy in range(4) for dz in range(2) if (dy, dz) != (0, 0)]

    barrier = pltpu.get_barrier_semaphore()
    peers = [(mate, c)]
    peers += [(row_peer(dy, dz), c) for dy, dz in offsets]
    peers += [(r, ((x + d) % 4) * 4 + zh) for d in range(1, 4)]
    peers += [(r, x * 4 + (zh + d) % 4) for d in range(1, 4)]
    for row, col in peers:
        pl.semaphore_signal(barrier, inc=1, device_id={"row": row, "col": col}, device_id_type=MESH)

    @pl.when(swap)
    def _():
        pl.semaphore_signal(barrier, inc=1, device_id={"row": c, "col": r}, device_id_type=MESH)

    zslab[...] = z_ref[:, pl.ds(pl.multiple_of(x * G, G), G)].T
    pl.semaphore_wait(barrier, len(peers) + swap.astype(jnp.int32))

    mine = zslab.at[rows(zh)]
    first = copy(mine, zct.at[rows(c)], st_sem.at[0], c, r)
    second = copy(h_ref.at[rows(c)], hc.at[rows(c)], st_sem.at[1], c, r)
    third = copy(c_ref, m, m_sem, c, r)

    @pl.when(swap)
    def _():
        first.start()
        second.start()
        third.start()

    @pl.when(jnp.logical_not(swap))
    def _():
        zct[rows(c)] = zslab[rows(zh)]
        hc[rows(c)] = h_ref[rows(c)]

    hi, lo = split(c_ref[...])
    ch[...] = hi
    cl[...] = lo

    def spread(buf, own, across, start):
        put(buf.at[rows(r)], buf.at[rows(r)], across.at[0], mate, c)
        for n, (dy, dz) in enumerate(offsets):
            put(buf.at[rows(r)], buf.at[rows(r)], own.at[n], row_peer(dy, dz), c)

    def forward(buf, own, across):
        for n, (dy, dz) in enumerate(offsets):
            here = buf.at[rows(row_from(dy, dz))]
            got(here, own.at[n])
            put(here, here, across.at[n + 1], mate, c)

    def collect(buf, across):
        got(buf.at[rows(mate)], across.at[0])
        for n, (dy, dz) in enumerate(offsets):
            got(buf.at[rows(row_from(dy, dz) + 1 - 2 * co)], across.at[n + 1])

    @pl.when(swap)
    def _():
        first.wait_recv()

    spread(zct, zg_sem, zc_sem, 0)
    forward(zct, zg_sem, zc_sem)
    collect(zct, zc_sem)

    for d in (1, 2, 3, 0):
        k = (x + d) % 4
        block = pl.ds(pl.multiple_of(k * G, G), G)
        pt[block] = dot3(split(zct[block]), (ch[...], cl[...]), NT)
        if d:
            for j in (1, 2, 3, 0):
                zj = (zh + j) % 4
                put(pt.at[rows(k * 4 + zj)], ra.at[d - 1, rows(zj)], ra_sem.at[d - 1, j], r, k * 4 + zh)
    for j in (1, 2, 3, 0):
        zj = (zh + j) % 4
        for d in range(3):
            got(ra.at[d, rows(zj)], ra_sem.at[d, j])
        total = pt[rows(x * 4 + zj)] + ra[0, rows(zj)] + ra[1, rows(zj)] + ra[2, rows(zj)]
        sb[j] = total
        if j:
            put(sb.at[j], rb.at[j], rb_sem.at[j], r, x * 4 + zj)
    for j in range(1, 4):
        got(rb.at[j], rb_sem.at[j])
    rt[rows(c)] = sb[0] + rb[1] + rb[2] + rb[3] - zslab[rows(zh)]

    own = rt.at[rows(c)]
    for j in range(1, 4):
        put(own, own, ag_sem.at[0, j], r, x * 4 + (zh + j) % 4)
    for d in range(1, 4):
        put(own, own, ag_sem.at[d, 0], r, ((x + d) % 4) * 4 + zh)
    for j in range(1, 4):
        here = rt.at[rows(x * 4 + (zh - j) % 4)]
        got(here, ag_sem.at[0, j])
        for d in range(1, 4):
            put(here, here, ag_sem.at[d, j], r, ((x + d) % 4) * 4 + zh)

    @pl.when(swap)
    def _():
        second.wait_recv()

    spread(hc, hg_sem, hcs_sem, 0)
    forward(hc, hg_sem, hcs_sem)
    collect(hc, hcs_sem)

    @pl.when(swap)
    def _():
        third.wait_recv()

    @pl.when(jnp.logical_not(swap))
    def _():
        m[...] = c_ref[...]

    across = m[...].T
    own_c = c_ref[...]
    symmetric = 0.5 * (own_c * own_c + across * across)
    relation = symmetric - dot3(split(h_ref[...]), split(hc[...]), NT)
    dc_ref[...] = 2.0 * own_c * relation

    slot = y * 2 + zl

    for d in range(4):
        k = (x - d) % 4
        if d:
            for j in range(4):
                got(rt.at[rows(k * 4 + (zh - j) % 4)], ag_sem.at[d, j])
        block = pl.ds(pl.multiple_of(k * G, G), G)
        tt[d] = dot3(split(rt[block]), (ch[...], cl[...]), NN)
        for j in range(2):
            put(tt.at[d, rows(j * 2 + 1 - co)], rc.at[d, j], rc_sem.at[d, j], mate, c)
    sent = []
    for d in range(4):
        k = (x - d) % 4
        for j in range(2):
            got(rc.at[d, j], rc_sem.at[d, j])
            target = k * 4 + j * 2 + co
            here = target == r
            se[d, j] = tt[d, rows(j * 2 + co)] + rc[d, j]
            one = copy(se.at[d, j], rd.at[slot], rd_sem.at[slot], target, c)
            sent.append((here, one))

            @pl.when(here)
            def _(d=d, j=j):
                rd[slot] = se[d, j]

            @pl.when(jnp.logical_not(here))
            def _(one=one):
                one.start()

    dc_ref[...] += dot3(split(rt[...].T), split(zct[...]), NN)

    for s in range(8):

        @pl.when(s != slot)
        def _(s=s):
            got(rd.at[s], rd_sem.at[s])

    tot[...] = ((rd[0] + rd[1]) + (rd[2] + rd[3])) + ((rd[4] + rd[5]) + (rd[6] + rd[7]))
    last = copy(tot, dzt, fin_sem, c, r)

    @pl.when(swap)
    def _():
        last.start()
        last.wait_recv()

    @pl.when(jnp.logical_not(swap))
    def _():
        dzt[...] = tot[...]

    dz_ref[...] = (dzt[...] - rt[rows(c)]).T

    for one in pending:
        one.wait_send()
    for here, one in sent:

        @pl.when(jnp.logical_not(here))
        def _(one=one):
            one.wait_send()

    @pl.when(swap)
    def _():
        for one in (first, second, third, last):
            one.wait_send()


def per_device(coeffs, features, factors):
    n, f = features.shape
    vmem = pl.BlockSpec(memory_space=pltpu.VMEM)
    dma = pltpu.SemaphoreType.DMA
    buf = lambda *shape: pltpu.VMEM(shape, F32)
    return pl.pallas_call(
        kernel,
        out_shape=(
            jax.ShapeDtypeStruct((n, n), F32),
            jax.ShapeDtypeStruct((n, S), F32),
        ),
        in_specs=[vmem] * 3,
        out_specs=(vmem, vmem),
        scratch_shapes=[
            buf(G, n), buf(f, n), buf(n, factors.shape[1]), buf(n, n),
            pltpu.VMEM((n, n), BF16), pltpu.VMEM((n, n), BF16),
            buf(f, n), buf(3, G, n), buf(4, S, n), buf(4, S, n), buf(f, n),
            buf(4, G, n), buf(4, 2, S, n), buf(4, 2, S, n), buf(8, S, n), buf(S, n), buf(S, n),
            dma((96,)), dma(()),
            dma((2,)), dma(()), dma((7,)), dma((8,)), dma((7,)), dma((8,)),
            dma((3, 4)), dma((4,)), dma((4, 4)), dma((4, 2)), dma((8,)), dma(()),
        ],
        compiler_params=pltpu.CompilerParams(
            collective_id=0, has_side_effects=True, vmem_limit_bytes=48 << 20
        ),
    )(coeffs, features, factors)


def solution(mesh):
    in_specs = (P("row", "col"), P("row", None), P("row", None))
    out_specs = (P("row", "col"), P("row", "col"))
    return jax.shard_map(
        per_device, mesh=mesh, in_specs=in_specs, out_specs=out_specs, check_vma=False
    )
```

time: 559 us -> 129 us (0.23)
  the two profiles are of different devices: /device:TPU:5 before, /device:TPU:16 now
where the time goes in v1:
time: 129 us
  Pallas kernels  123 us (95%)
  local copies, waits for them, and re-layouts  5.19 us (4%)
    pallas_call x1, Pallas kernels, per_device(): pl.pallas_call(kernel, out_shape=(jax.ShapeDtypeStruct((n, n), F32), jax....  123 us
    unnamed x7, local copies, waits for them, and re-layouts  4.45 us

profile of v1, /device:TPU:16, one launch (start us, length us, event | category | flops | bytes accessed | tf_op | source)
XLA Modules:
  0.0 128.6 jit_solution(11809919228415983712)
XLA Ops:
  0.6 0.0 copy-start
  0.6 1.2 copy-done
  1.9 0.0 copy-start.1
  1.9 1.2 copy-done.1
  3.1 0.0 copy-start.2
  3.1 1.0 copy-done.2
  4.1 122.7 %shard_map.50 = (f32[512,512]{1,0:T(8,128)S(1)}, f32[512,32]{1,0:T(8,128)S(1)}) custom-call(f32[512,512]{1,0:T(8,128)S(1)} %copy-done, f32[512,512]{1,0:T(8,128)S(1)} %copy-done.1, f32[512,256]{1,0:T(8,128)S(1)} %copy-done.2), custom_call_target="tpu_custom_call" | custom-call | tf_op jit(solution)/shard_map/pallas_call | solution.py:258
  126.9 0.7 copy.5
  127.6 1.0 copy.7
Async XLA Ops:
  0.6 1.2 copy-start
  1.9 1.2 copy-start.1
  3.1 1.0 copy-start.2

commit v2 on v1

v2 whole, which is shorter than its diff:
```python
import functools

import jax
import jax.numpy as jnp
from jax import lax
from jax.experimental import pallas as pl
from jax.experimental.pallas import tpu as pltpu
from jax.sharding import PartitionSpec as P

F32, BF16 = jnp.float32, jnp.bfloat16
MESH = pl.DeviceIdType.MESH
NN = (((1,), (0,)), ((), ()))
NT = (((1,), (1,)), ((), ()))
TP = '0237'
MP = '6789'
HS = '1'
HQ = '6'
HF = '8'
S = 32
G = 128


def split(a):
    hi = a.astype(BF16)
    return hi, (a - hi.astype(F32)).astype(BF16)


def dot3(a, b, dims):
    ah, al = a
    bh, bl = b
    dot = functools.partial(lax.dot_general, dimension_numbers=dims, preferred_element_type=F32)
    return dot(ah, bh) + (dot(ah, bl) + dot(al, bh))


def kernel(
    c_ref, z_ref, h_ref, dc_ref, dz_ref,
    cv, hv, zfirst, zown, zslab, zsub, zct, hc, m, relay, ch, cl, pt, ra, sb, rb, rt, tt, rc, se, rd, tot, dzt,
    send, rsend, in_sem,
    st_sem, m_sem, y_sem, zg_sem, zc_sem, hg_sem, hcs_sem, ra_sem, rb_sem, ag_sem, rc_sem, rd_sem, fin_sem,
):
    r, c = lax.axis_index("row"), lax.axis_index("col")
    y, zl, co = r // 4, (r // 2) % 2, r % 2
    x, zh = c // 4, c % 4
    swap = r != c
    diagonal = x == y
    far = (x - y + 4) % 4 == 2
    mate = r + 1 - 2 * co
    turn = (x + y) % 4

    def rows(start, size=S):
        return pl.ds(pl.multiple_of(start * S, S), size)

    def group(k):
        return pl.ds(pl.multiple_of(k * G, G), G)

    def row_peer(dy, dz):
        return ((y + dy) % 4) * 4 + ((zl + dz) % 2) * 2 + co

    def slice_from(dy, dz, core):
        return rows(((y - dy + x + 4) % 4) * 4 + ((zl + dz) % 2) * 2 + core)

    count = [0]
    pending = []

    def copy(src, dst, sem, row, col):
        n = count[0]
        count[0] += 1
        return pltpu.make_async_remote_copy(
            src_ref=src, dst_ref=dst, send_sem=send.at[n], recv_sem=sem,
            device_id={"row": row, "col": col}, device_id_type=MESH,
        )

    def put(src, dst, sem, row, col):
        one = copy(src, dst, sem, row, col)
        one.start()
        pending.append((None, one))

    def put_if(where, src, dst, sem, row, col):
        one = copy(src, dst, sem, row, col)

        @pl.when(where)
        def _():
            one.start()

        pending.append((where, one))

    def got(dst, sem):
        pltpu.make_async_remote_copy(
            src_ref=dst, dst_ref=dst, send_sem=rsend, recv_sem=sem,
            device_id={"row": mate, "col": c}, device_id_type=MESH,
        ).wait_recv()

    offsets = [(0, 1), (1, 0), (1, 1), (3, 0), (3, 1), (2, 0), (2, 1)]

    lanes = lambda k: pl.ds(pl.multiple_of(k * G, G), G)
    loads = [
        pltpu.make_async_copy(z_ref.at[:, lanes(turn)], zfirst, in_sem.at[0]),
        pltpu.make_async_copy(c_ref, cv, in_sem.at[1]),
        pltpu.make_async_copy(z_ref.at[:, lanes(x)], zown, in_sem.at[2]),
        pltpu.make_async_copy(h_ref, hv, in_sem.at[3]),
    ]
    for one in loads:
        one.start()

    barrier = pltpu.get_barrier_semaphore()

    def greet(row, col):
        pl.semaphore_signal(barrier, inc=1, device_id={"row": row, "col": col}, device_id_type=MESH)

    @pl.when(swap)
    def _():
        greet(c, r)

    @pl.when(diagonal)
    def _():
        greet(((y + 2) % 4) * 4 + zh, r)

    peers = [(mate, c)]
    peers += [(row_peer(dy, dz), c) for dy, dz in offsets]
    peers += [(r, ((x + d) % 4) * 4 + zh) for d in range(1, 4)]
    peers += [(r, x * 4 + (zh + d) % 4) for d in range(1, 4)]
    for row, col in peers:
        greet(row, col)
    loads[0].wait()
    zslab[...] = zfirst[...].T
    pl.semaphore_wait(barrier, len(peers) + swap.astype(jnp.int32) + far.astype(jnp.int32))

    mine = rows(turn * 4 + zh)
    ours = slice_from(0, 0, co)
    first = copy(zslab.at[rows(zh)], zct.at[mine], st_sem.at[0], c, r)
    second = copy(h_ref.at[mine], hc.at[mine], st_sem.at[1], c, r)

    @pl.when(swap)
    def _():
        first.start()

    @pl.when(jnp.logical_not(swap))
    def _():
        zct[mine] = zslab[rows(zh)]

    near = jnp.logical_and(swap, jnp.logical_not(far))
    hop = []

    def mirror_out(i):
        part = pl.ds(i * G, G)
        put_if(near, c_ref.at[part], m.at[part], m_sem.at[i], c, r)
        put_if(far, c_ref.at[part], relay.at[part], y_sem.at[i], c, x * 4 + r % 4)

    def mirror_pass(i):
        part = pl.ds(i * G, G)
        one = copy(relay.at[part], m.at[part], m_sem.at[i], r, ((y + 2) % 4) * 4 + zh)

        @pl.when(diagonal)
        def _():
            got(relay.at[part], y_sem.at[i])
            one.start()

        pending.append((diagonal, one))

    def swap_factors():
        @pl.when(swap)
        def _():
            second.start()

    def point(name):
        if name == HS:
            swap_factors()
        if name == HQ:
            @pl.when(swap)
            def _():
                second.wait_recv()
            spread(hc, hg_sem, hcs_sem)
        if name == HF:
            for n in range(7):
                forward(hc, hg_sem, hcs_sem, n)
        for i in range(4):
            if TP[i] == name:
                mirror_out(i)
        for i in range(4):
            if MP[i] == name:
                mirror_pass(i)

    def spread(buf, own, across):
        put(buf.at[ours], buf.at[ours], across.at[0], mate, c)
        for n, (dy, dz) in enumerate(offsets):
            put(buf.at[ours], buf.at[ours], own.at[n], row_peer(dy, dz), c)

    def forward(buf, own, across, n):
        here = buf.at[slice_from(*offsets[n], co)]
        got(here, own.at[n])
        put(here, here, across.at[n + 1], mate, c)

    def collect(buf, across, n):
        got(buf.at[slice_from(*((0, 0) if n == 0 else offsets[n - 1]), 1 - co)], across.at[n])

    point('0')
    loads[1].wait()
    hi, lo = split(cv[...])
    ch[...] = hi
    cl[...] = lo
    loads[2].wait()
    zsub[...] = zown[...].T

    loads[3].wait()

    @pl.when(jnp.logical_not(swap))
    def _():
        hc[mine] = hv[mine]

    @pl.when(swap)
    def _():
        first.wait_recv()

    spread(zct, zg_sem, zc_sem)
    point('1')

    for step, dy in enumerate((0, 1, 3, 2)):
        for n in ((0,), (1, 2), (3, 4), (5, 6))[step]:
            forward(zct, zg_sem, zc_sem, n)
        for n in ((0, 1), (2, 3), (4, 5), (6, 7))[step]:
            collect(zct, zc_sem, n)
        k = (y - dy + x + 4) % 4
        pt[step] = dot3(split(zct[group(k)]), (ch[...], cl[...]), NT)
        for j in (1, 2, 3, 0):
            zj = (zh + j) % 4
            put_if(k != x, pt.at[step, rows(zj)], ra.at[x, rows(zj)], ra_sem.at[x, j], r, k * 4 + zh)

        @pl.when(k == x)
        def _(step=step):
            ra[x] = pt[step]

        point('2345'[step])


    for j in (1, 2, 3, 0):
        zj = (zh + j) % 4
        for d in range(1, 4):
            source = (x + d) % 4
            got(ra.at[source, rows(zj)], ra_sem.at[source, j])
        total = (ra[0, rows(zj)] + ra[1, rows(zj)]) + (ra[2, rows(zj)] + ra[3, rows(zj)])
        sb[j] = total
        if j:
            put(sb.at[j], rb.at[j], rb_sem.at[j], r, x * 4 + zj)
    point('6')
    for j in range(1, 4):
        got(rb.at[j], rb_sem.at[j])
    rt[rows(c)] = sb[0] + rb[1] + rb[2] + rb[3] - zsub[rows(zh)]

    own = rt.at[rows(c)]
    for j in range(1, 4):
        put(own, own, ag_sem.at[0, j], r, x * 4 + (zh + j) % 4)
    for d in range(1, 4):
        put(own, own, ag_sem.at[d, 0], r, ((x + d) % 4) * 4 + zh)
    point('7')
    for j in range(1, 4):
        here = rt.at[rows(x * 4 + (zh - j + 4) % 4)]
        got(here, ag_sem.at[0, j])
        for d in range(1, 4):
            put(here, here, ag_sem.at[d, j], r, ((x + d) % 4) * 4 + zh)

    point('8')

    slot = y * 2 + zl
    def reduce_row(d):
        k = (x - d + 4) % 4
        for j in range(2):
            got(rc.at[d, j], rc_sem.at[d, j])
            target = k * 4 + j * 2 + co
            se[d, j] = tt[d, rows(j * 2 + co)] + rc[d, j]
            put_if(target != r, se.at[d, j], rd.at[slot], rd_sem.at[slot], target, c)

            @pl.when(target == r)
            def _():
                rd[slot] = se[d, j]

    for d in range(4):
        k = (x - d + 4) % 4
        if d:
            for j in range(4):
                got(rt.at[rows(k * 4 + (zh - j + 4) % 4)], ag_sem.at[d, j])
        tt[d] = dot3(split(rt[group(k)]), (ch[...], cl[...]), NN)
        for j in range(2):
            put(tt.at[d, rows(j * 2 + 1 - co)], rc.at[d, j], rc_sem.at[d, j], mate, c)
        if d == 0:
            for n in range(8):
                collect(hc, hcs_sem, n)
            own_c = cv[...]
            dc_ref[...] = own_c * own_c - 2.0 * dot3(split(hv[...]), split(hc[...]), NT)
        if d:
            reduce_row(d - 1)
        point('9abc'[d])
    reduce_row(3)
    point('d')

    outer = dot3(split(rt[...].T), split(zct[...]), NN)
    dc_ref[...] = outer + cv[...] * dc_ref[...]

    for s in range(8):

        @pl.when(s != slot)
        def _(s=s):
            got(rd.at[s], rd_sem.at[s])

    tot[...] = ((rd[0] + rd[1]) + (rd[2] + rd[3])) + ((rd[4] + rd[5]) + (rd[6] + rd[7]))
    put_if(swap, tot, dzt, fin_sem, c, r)

    @pl.when(swap)
    def _():
        for i in range(4):
            got(m.at[pl.ds(i * G, G)], m_sem.at[i])

    @pl.when(jnp.logical_not(swap))
    def _():
        m[...] = cv[...]

    across = m[...].T
    dc_ref[...] += cv[...] * (across * across)

    @pl.when(swap)
    def _():
        got(dzt, fin_sem)

    @pl.when(jnp.logical_not(swap))
    def _():
        dzt[...] = tot[...]

    dz_ref[...] = (dzt[...] - rt[rows(c)]).T

    for where, one in [(swap, first), (swap, second)] + pending:
        if where is None:
            one.wait_send()
        else:

            @pl.when(where)
            def _(one=one):
                one.wait_send()


def per_device(coeffs, features, factors):
    n, f = features.shape
    k = factors.shape[1]
    vmem = pl.BlockSpec(memory_space=pltpu.VMEM)
    dma = pltpu.SemaphoreType.DMA
    buf = lambda *shape: pltpu.VMEM(shape, F32)
    return pl.pallas_call(
        kernel,
        out_shape=(
            jax.ShapeDtypeStruct((n, n), F32),
            jax.ShapeDtypeStruct((n, S), F32),
        ),
        in_specs=[pl.BlockSpec(memory_space=pl.ANY)] * 3,
        out_specs=(vmem, vmem),
        scratch_shapes=[
            buf(n, n), buf(n, k), buf(n, G), buf(n, G), buf(G, n), buf(G, n), buf(f, n), buf(n, k), buf(n, n), buf(n, n),
            pltpu.VMEM((n, n), BF16), pltpu.VMEM((n, n), BF16),
            buf(4, G, n), buf(4, G, n), buf(4, S, n), buf(4, S, n), buf(f, n),
            buf(4, G, n), buf(4, 2, S, n), buf(4, 2, S, n), buf(8, S, n), buf(S, n), buf(S, n),
            dma((128,)), dma(()), dma((4,)),
            dma((2,)), dma((4,)), dma((4,)), dma((7,)), dma((8,)), dma((7,)), dma((8,)),
            dma((4, 4)), dma((4,)), dma((4, 4)), dma((4, 2)), dma((8,)), dma(()),
        ],
        compiler_params=pltpu.CompilerParams(
            collective_id=0, has_side_effects=True, vmem_limit_bytes=48 << 20
        ),
    )(coeffs, features, factors)


def solution(mesh):
    in_specs = (P("row", "col"), P("row", None), P("row", None))
    out_specs = (P("row", "col"), P("row", "col"))
    return jax.shard_map(
        per_device, mesh=mesh, in_specs=in_specs, out_specs=out_specs, check_vma=False
    )
```

time: 129 us -> 98.3 us (0.76)
  the two profiles are of different devices: /device:TPU:16 before, /device:TPU:5 now
where the time goes in v2:
time: 98.3 us; the launch traced here: 96.4 us
  Pallas kernels  90.5 us (92%)
  local copies, waits for them, and re-layouts  5.19 us (5%)
    pallas_call x1, Pallas kernels, per_device(): pl.pallas_call(kernel, out_shape=(jax.ShapeDtypeStruct((n, n), F32), jax....  90.5 us
    unnamed x7, local copies, waits for them, and re-layouts  4.45 us

profile of v2, /device:TPU:5, one launch (start us, length us, event | category | flops | bytes accessed | tf_op | source)
XLA Modules:
  0.0 96.4 jit_solution(13777537788946156890)
XLA Ops:
  0.6 0.0 copy-start
  0.6 1.2 %copy-done = f32[512,512]{1,0:T(8,128)S(1)} copy-done((f32[512,512]{1,0:T(8,128)S(1)}, f32[512,512]{1,0:T(8,128)}, u32[]{:S(2)}) %copy-start) | copy-done | bytes 1048600
  1.9 0.0 copy-start.1
  1.9 1.2 %copy-done.1 = f32[512,512]{1,0:T(8,128)S(1)} copy-done((f32[512,512]{1,0:T(8,128)S(1)}, f32[512,512]{1,0:T(8,128)}, u32[]{:S(2)}) %copy-start.1) | copy-done | bytes 1048600
  3.1 0.0 copy-start.2
  3.1 1.0 %copy-done.2 = f32[512,256]{1,0:T(8,128)S(1)} copy-done((f32[512,256]{1,0:T(8,128)S(1)}, f32[512,256]{1,0:T(8,128)}, u32[]{:S(2)}) %copy-start.2) | copy-done | bytes 524312
  4.1 90.5 %shard_map.50 = (f32[512,512]{1,0:T(8,128)S(1)}, f32[512,32]{1,0:T(8,128)S(1)}) custom-call(f32[512,512]{1,0:T(8,128)S(1)} %copy-done, f32[512,512]{1,0:T(8,128)S(1)} %copy-done.1, f32[512,256]{1,0:T(8,128)S(1)} %copy-done.2), custom_call_target="tpu_custom_call" | custom-call | tf_op jit(solution)/shard_map/pallas_call | solution.py:345
  94.7 0.7 copy.5
  95.4 1.0 %copy.7 = f32[512,512]{1,0:T(8,128)} copy(f32[512,512]{1,0:T(8,128)S(1)} %get-tuple-element.6) | data formatting | bytes 2097152
Async XLA Ops:
  0.6 1.2 %copy-start = (f32[512,512]{1,0:T(8,128)S(1)}, f32[512,512]{1,0:T(8,128)}, u32[]{:S(2)}) copy-start(f32[512,512]{1,0:T(8,128)} %c_ref.1) | copy-start | bytes 3145732
  1.9 1.2 %copy-start.1 = (f32[512,512]{1,0:T(8,128)S(1)}, f32[512,512]{1,0:T(8,128)}, u32[]{:S(2)}) copy-start(f32[512,512]{1,0:T(8,128)} %z_ref.1) | copy-start | bytes 3145732
  3.1 1.0 %copy-start.2 = (f32[512,256]{1,0:T(8,128)S(1)}, f32[512,256]{1,0:T(8,128)}, u32[]{:S(2)}) copy-start(f32[512,256]{1,0:T(8,128)} %h_ref.1) | copy-start | bytes 1572868

commit v3 on v2

v3 whole, which is shorter than its diff:
```python
import functools

import jax
import jax.numpy as jnp
from jax import lax
from jax.experimental import pallas as pl
from jax.experimental.pallas import tpu as pltpu
from jax.sharding import PartitionSpec as P

F32, BF16 = jnp.float32, jnp.bfloat16
MESH = pl.DeviceIdType.MESH
NN = (((1,), (0,)), ((), ()))
NT = (((1,), (1,)), ((), ()))
SP = 0
REL = 1
DIR = 1
TP = '01235678'
MP = '2345789a'
HS = '1'
HQ = '5'
HF = '6'
HG = 'a'
S = 32
PIECE = 64
T = 16
G = 128


def split(a):
    hi = a.astype(BF16)
    return hi, (a - hi.astype(F32)).astype(BF16)


def dot3(a, b, dims):
    ah, al = a
    bh, bl = b
    dot = functools.partial(lax.dot_general, dimension_numbers=dims, preferred_element_type=F32)
    return dot(ah, bh) + (dot(ah, bl) + dot(al, bh))


def kernel(
    c_ref, z_ref, h_ref, dc_ref, dz_ref,
    cv, hv, zfirst, zown, zslab, zsub, zct, hc, m, relay, ch, cl, th, tl, pt, ra, sb, rb, rt, tt, rc, se, rd, tot, dzt,
    send, rsend, in_sem,
    st_sem, h_sem, m_sem, y_sem, zg_sem, zc_sem, hg_sem, hcs_sem, ra_sem, rb_sem, ag_sem, rc_sem, rd_sem, fin_sem,
):
    r, c = lax.axis_index("row"), lax.axis_index("col")
    y, zl, co = r // 4, (r // 2) % 2, r % 2
    x, zh = c // 4, c % 4
    swap = r != c
    diagonal = x == y if REL else x > 99
    far = (x - y + 4) % 4 == 2 if REL else x > 99
    near = jnp.logical_and(swap, jnp.logical_not(far))
    mate = r + 1 - 2 * co
    turn = (x + y) % 4

    def rows(start, size):
        return pl.ds(pl.multiple_of(start * size, size), size)

    def share(start):
        return rows(start, T)

    def row_peer(dy, dz):
        return ((y + dy) % 4) * 4 + ((zl + dz) % 2) * 2 + co

    def slice_from(dy, dz, core):
        return ((y - dy + x + 4) % 4) * 4 + ((zl + dz) % 2) * 2 + core

    count = [0]
    pending = []

    def copy(src, dst, sem, row, col):
        n = count[0]
        count[0] += 1
        return pltpu.make_async_remote_copy(
            src_ref=src, dst_ref=dst, send_sem=send.at[n], recv_sem=sem,
            device_id={"row": row, "col": col}, device_id_type=MESH,
        )

    def put(src, dst, sem, row, col):
        one = copy(src, dst, sem, row, col)
        one.start()
        pending.append((None, one))

    def put_if(where, src, dst, sem, row, col):
        one = copy(src, dst, sem, row, col)

        @pl.when(where)
        def _():
            one.start()

        pending.append((where, one))

    def got(dst, sem):
        pltpu.make_async_remote_copy(
            src_ref=dst, dst_ref=dst, send_sem=rsend, recv_sem=sem,
            device_id={"row": mate, "col": c}, device_id_type=MESH,
        ).wait_recv()

    def got_if(where, dst, sem):
        @pl.when(where)
        def _():
            got(dst, sem)

    lanes = lambda k: pl.ds(pl.multiple_of(k * G, G), G)
    loads = [
        pltpu.make_async_copy(z_ref.at[:, lanes(turn)], zfirst, in_sem.at[0]),
        pltpu.make_async_copy(c_ref, cv, in_sem.at[1]),
        pltpu.make_async_copy(z_ref.at[:, lanes(x)], zown, in_sem.at[2]),
        pltpu.make_async_copy(h_ref, hv, in_sem.at[3]),
    ]
    for one in loads:
        one.start()

    barrier = pltpu.get_barrier_semaphore()

    def greet(row, col):
        pl.semaphore_signal(barrier, inc=1, device_id={"row": row, "col": col}, device_id_type=MESH)

    @pl.when(swap)
    def _():
        greet(c, r)

    @pl.when(diagonal)
    def _():
        greet(((y + 2) % 4) * 4 + zh, r)

    peers = [(mate, c)]
    peers += [(row_peer(dy, dz), c) for dy in range(4) for dz in range(2) if dy or dz]
    peers += [(r, ((x + d) % 4) * 4 + zh) for d in range(1, 4)]
    peers += [(r, x * 4 + (zh + d) % 4) for d in range(1, 4)]
    for row, col in peers:
        greet(row, col)
    loads[0].wait()
    zslab[...] = zfirst[...].T
    pl.semaphore_wait(barrier, len(peers) + swap.astype(jnp.int32) + far.astype(jnp.int32))

    mine = turn * 4 + zh
    for h in range(2):
        put_if(swap, zslab.at[share(zh * 2 + h)], zct.at[h, share(mine)], st_sem.at[h], c, r)

        @pl.when(jnp.logical_not(swap))
        def _(h=h):
            zct[h, share(mine)] = zslab[share(zh * 2 + h)]

    def mirror_out(i):
        part = pl.ds(i * PIECE, PIECE)
        put_if(near, c_ref.at[part], m.at[part], m_sem.at[i], c, r)
        put_if(far, c_ref.at[part], relay.at[part], y_sem.at[i], c, x * 4 + r % 4)

    def mirror_pass(i):
        part = pl.ds(i * PIECE, PIECE)
        got_if(diagonal, relay.at[part], y_sem.at[i])
        put_if(diagonal, relay.at[part], m.at[part], m_sem.at[i], r, ((y + 2) % 4) * 4 + zh)

    def spread(at, own, across, direct=False):
        here = at(slice_from(0, 0, co))
        put(here, here, across.at[0, 0], mate, c)
        put(here, here, own.at[0, 1], row_peer(0, 1), c)
        for dy in (1, 3, 2):
            put(here, here, own.at[dy, 0], row_peer(dy, 0), c)
        if direct:
            for dy in (1, 3, 2):
                put(here, here, own.at[dy, 1], row_peer(dy, 1), c)

    def forward(at, own, across, dy, dz, direct=False):
        here = at(slice_from(dy, dz, co))
        got(here, own.at[dy, dz])
        put(here, here, across.at[dy, dz], mate, c)
        if dy == 0 and not direct:
            for to in (1, 3, 2):
                put(here, here, own.at[to, 1], row_peer(to, 0), c)

    def collect(at, across, dy):
        for dz in range(2):
            got(at(slice_from(dy, dz, 1 - co)), across.at[dy, dz])

    factor = lambda s: hc.at[rows(s, S)]
    feature = [lambda s, h=h: zct.at[h, share(s)] for h in range(2)]

    def point(name):
        if name == HS:
            put_if(swap, h_ref.at[rows(mine, S)], hc.at[rows(mine, S)], h_sem, c, r)
        if name == HQ:
            got_if(swap, hc.at[rows(mine, S)], h_sem)
            spread(factor, hg_sem, hcs_sem)
        if name == HF:
            forward(factor, hg_sem, hcs_sem, 0, 1)
        if name == HG:
            for dy, dz in ((1, 0), (3, 0), (2, 0), (1, 1), (3, 1), (2, 1)):
                forward(factor, hg_sem, hcs_sem, dy, dz)
        for i in range(8):
            if TP[i] == name:
                mirror_out(i)
        for i in range(8):
            if MP[i] == name:
                mirror_pass(i)

    point("0")
    loads[1].wait()
    hi, lo = split(cv[...])
    ch[...] = hi
    cl[...] = lo
    hi, lo = split(cv[...].T)
    th[...] = hi
    tl[...] = lo
    loads[2].wait()
    zsub[...] = zown[...].T
    loads[3].wait()

    @pl.when(jnp.logical_not(swap))
    def _():
        hc[rows(mine, S)] = hv[rows(mine, S)]

    def begin(h):
        got_if(swap, zct.at[h, share(mine)], st_sem.at[h])
        spread(feature[h], zg_sem.at[h], zc_sem.at[h], h < DIR)

    begin(0)
    if SP == 0:
        begin(1)
    point("1")

    def product(h, step, dy):
        collect(feature[h], zc_sem.at[h], dy)
        k = (y - dy + x + 4) % 4
        pt[h, step] = dot3(split(zct[h, rows(k, 4 * T)]), (th[...], tl[...]), NN)
        for j in (1, 2, 3, 0):
            zj = (zh + j) % 4
            put_if(k != x, pt.at[h, step, share(zj)], ra.at[h, x, share(zj)], ra_sem.at[h, x, j], r, k * 4 + zh)

        @pl.when(k == x)
        def _():
            ra[h, x] = pt[h, step]

    def products(h):
        pair = feature[h], zg_sem.at[h], zc_sem.at[h]
        forward(*pair, 0, 1, h < DIR)
        if h == 0 and SP == 1:
            begin(1)
        product(h, 0, 0)
        for dy, dz in ((1, 0), (3, 0), (1, 1), (3, 1)):
            forward(*pair, dy, dz)
        if h == 0 and SP == 2:
            begin(1)
        product(h, 1, 1 + 2 * co)
        product(h, 2, 3 - 2 * co)
        point("24"[h])
        for dz in range(2):
            forward(*pair, 2, dz)
        if h == 0 and SP == 3:
            begin(1)
        product(h, 3, 2)
        point("35"[h])

    def sum_x(h):
        for j in (1, 2, 3, 0):
            zj = (zh + j) % 4
            for d in range(1, 4):
                source = (x + d) % 4
                got(ra.at[h, source, share(zj)], ra_sem.at[h, source, j])
            at = share(zj)
            sb[h, j] = (ra[h, 0, at] + ra[h, 1, at]) + (ra[h, 2, at] + ra[h, 3, at])
            if j:
                put(sb.at[h, j], rb.at[h, j], rb_sem.at[h, j], r, x * 4 + zj)

    def sum_z(h):
        for j in range(1, 4):
            got(rb.at[h, j], rb_sem.at[h, j])
        rt[h, share(c)] = sb[h, 0] + rb[h, 1] + rb[h, 2] + rb[h, 3] - zsub[share(zh * 2 + h)]
        own = rt.at[h, share(c)]
        for j in range(1, 4):
            put(own, own, ag_sem.at[h, 0, j], r, x * 4 + (zh + j) % 4)
        for d in (1, 3, 2):
            put(own, own, ag_sem.at[h, d, 0], r, ((x + d) % 4) * 4 + zh)

    def spread_x(h):
        for j in range(1, 4):
            here = rt.at[h, share(x * 4 + (zh - j + 4) % 4)]
            got(here, ag_sem.at[h, 0, j])
            for d in (1, 3, 2):
                put(here, here, ag_sem.at[h, d, j], r, ((x + d) % 4) * 4 + zh)

    products(0)
    products(1)
    sum_x(0)
    sum_z(0)
    point("6")
    sum_x(1)
    spread_x(0)
    point("7")
    sum_z(1)
    spread_x(1)
    point("8")

    slot = y * 2 + zl

    def term(h, d):
        k = (x - d + 4) % 4
        if d:
            for j in range(4):
                got(rt.at[h, share(k * 4 + (zh - j + 4) % 4)], ag_sem.at[h, d, j])
        tt[h, d] = dot3(split(rt[h, rows(k, 4 * T)]), (ch[...], cl[...]), NN)
        for j in range(2):
            put(tt.at[h, d, share(j * 2 + 1 - co)], rc.at[h, d, j], rc_sem.at[h, d, j], mate, c)

    def sum_core(h, d):
        k = (x - d + 4) % 4
        for j in range(2):
            got(rc.at[h, d, j], rc_sem.at[h, d, j])
            target = k * 4 + j * 2 + co
            se[h, d, j] = tt[h, d, share(j * 2 + co)] + rc[h, d, j]
            put_if(target != r, se.at[h, d, j], rd.at[h, slot], rd_sem.at[h, slot], target, c)

            @pl.when(target == r)
            def _():
                rd[h, slot] = se[h, d, j]

    def sum_row(h):
        for s in range(8):
            got_if(s != slot, rd.at[h, s], rd_sem.at[h, s])
        tot[h] = ((rd[h, 0] + rd[h, 1]) + (rd[h, 2] + rd[h, 3])) + ((rd[h, 4] + rd[h, 5]) + (rd[h, 6] + rd[h, 7]))
        put_if(swap, tot.at[h], dzt.at[share(h)], fin_sem.at[h], c, r)

        @pl.when(jnp.logical_not(swap))
        def _():
            dzt[share(h)] = tot[h]

    term(0, 0)
    term(1, 0)
    sum_core(0, 0)
    sum_core(1, 0)
    for h in range(2):
        for d in (1, 3, 2):
            term(h, d)
        for d in (1, 3, 2):
            sum_core(h, d)
        point("9a"[h])
    sum_row(0)
    point("b")
    sum_row(1)
    point("c")
    for dy in range(4):
        collect(factor, hcs_sem, dy)
    own_c = cv[...]
    dc_ref[...] = own_c * own_c - 2.0 * dot3(split(hv[...]), split(hc[...]), NT)
    outer = dot3(split(rt[0].T), split(zct[0]), NN) + dot3(split(rt[1].T), split(zct[1]), NN)
    dc_ref[...] = outer + cv[...] * dc_ref[...]

    for i in range(8):
        got_if(swap, m.at[pl.ds(i * PIECE, PIECE)], m_sem.at[i])

    @pl.when(jnp.logical_not(swap))
    def _():
        m[...] = cv[...]

    across = m[...].T
    dc_ref[...] += cv[...] * (across * across)

    for h in range(2):
        got_if(swap, dzt.at[share(h)], fin_sem.at[h])
        rs = rt[h, share(c)]
        dzt[share(h)] = dzt[share(h)] - rs
    dz_ref[...] = dzt[...].T

    for where, one in pending:
        if where is None:
            one.wait_send()
        else:

            @pl.when(where)
            def _(one=one):
                one.wait_send()


def per_device(coeffs, features, factors):
    n, f = features.shape
    k = factors.shape[1]
    vmem = pl.BlockSpec(memory_space=pltpu.VMEM)
    dma = pltpu.SemaphoreType.DMA
    buf = lambda *shape: pltpu.VMEM(shape, F32)
    half = lambda *shape: pltpu.VMEM(shape, BF16)
    return pl.pallas_call(
        kernel,
        out_shape=(
            jax.ShapeDtypeStruct((n, n), F32),
            jax.ShapeDtypeStruct((n, S), F32),
        ),
        in_specs=[pl.BlockSpec(memory_space=pl.ANY)] * 3,
        out_specs=(vmem, vmem),
        scratch_shapes=[
            buf(n, n), buf(n, k), buf(n, G), buf(n, G), buf(G, n), buf(G, n), buf(2, f // 2, n), buf(n, k),
            buf(n, n), buf(n, n), half(n, n), half(n, n), half(n, n), half(n, n),
            buf(2, 4, 4 * T, n), buf(2, 4, 4 * T, n), buf(2, 4, T, n), buf(2, 4, T, n), buf(2, f // 2, n),
            buf(2, 4, 4 * T, n), buf(2, 4, 2, T, n), buf(2, 4, 2, T, n), buf(2, 8, T, n), buf(2, T, n), buf(S, n),
            dma((192,)), dma(()), dma((4,)),
            dma((2,)), dma(()), dma((8,)), dma((8,)), dma((2, 4, 2)), dma((2, 4, 2)), dma((4, 2)), dma((4, 2)),
            dma((2, 4, 4)), dma((2, 4)), dma((2, 4, 4)), dma((2, 4, 2)), dma((2, 8)), dma((2,)),
        ],
        compiler_params=pltpu.CompilerParams(
            collective_id=0, has_side_effects=True, vmem_limit_bytes=48 << 20
        ),
    )(coeffs, features, factors)


def solution(mesh):
    in_specs = (P("row", "col"), P("row", None), P("row", None))
    out_specs = (P("row", "col"), P("row", "col"))
    return jax.shard_map(
        per_device, mesh=mesh, in_specs=in_specs, out_specs=out_specs, check_vma=False
    )
```

time: 98.3 us -> 94.5 us (0.961); the launches traced: 96.4 us -> 94.3 us
  Pallas kernels: 90.5 us -> 88.4 us
    pallas_call x1, Pallas kernels: 90.5 us -> 88.4 us  [per_device(): pl.pallas_call(kernel, out_shape=(jax.ShapeDtypeStruct((n, n), F32), jax....]
where the time goes in v3:
time: 94.5 us; the launch traced here: 94.3 us
  Pallas kernels  88.4 us (94%)
  local copies, waits for them, and re-layouts  5.19 us (5%)
    pallas_call x1, Pallas kernels, per_device(): pl.pallas_call(kernel, out_shape=(jax.ShapeDtypeStruct((n, n), F32), jax....  88.4 us
    unnamed x7, local copies, waits for them, and re-layouts  4.45 us

profile of v3, /device:TPU:5, one launch (start us, length us, event | category | flops | bytes accessed | tf_op | source)
XLA Modules:
  0.0 94.3 jit_solution(16167990382935412987)
XLA Ops:
  0.6 0.0 copy-start
  0.6 1.2 %copy-done = f32[512,512]{1,0:T(8,128)S(1)} copy-done((f32[512,512]{1,0:T(8,128)S(1)}, f32[512,512]{1,0:T(8,128)}, u32[]{:S(2)}) %copy-start) | copy-done | bytes 1048600
  1.9 0.0 copy-start.1
  1.9 1.2 %copy-done.1 = f32[512,512]{1,0:T(8,128)S(1)} copy-done((f32[512,512]{1,0:T(8,128)S(1)}, f32[512,512]{1,0:T(8,128)}, u32[]{:S(2)}) %copy-start.1) | copy-done | bytes 1048600
  3.1 0.0 copy-start.2
  3.1 1.0 %copy-done.2 = f32[512,256]{1,0:T(8,128)S(1)} copy-done((f32[512,256]{1,0:T(8,128)S(1)}, f32[512,256]{1,0:T(8,128)}, u32[]{:S(2)}) %copy-start.2) | copy-done | bytes 524312
  4.1 88.4 %shard_map.50 = (f32[512,512]{1,0:T(8,128)S(1)}, f32[512,32]{1,0:T(8,128)S(1)}) custom-call(f32[512,512]{1,0:T(8,128)S(1)} %copy-done, f32[512,512]{1,0:T(8,128)S(1)} %copy-done.1, f32[512,256]{1,0:T(8,128)S(1)} %copy-done.2), custom_call_target="tpu_custom_call" | custom-call | tf_op jit(solution)/shard_map/pallas_call | solution.py:383
  92.5 0.7 copy.5
  93.3 1.0 %copy.7 = f32[512,512]{1,0:T(8,128)} copy(f32[512,512]{1,0:T(8,128)S(1)} %get-tuple-element.6) | data formatting | bytes 2097152
Async XLA Ops:
  0.6 1.2 %copy-start = (f32[512,512]{1,0:T(8,128)S(1)}, f32[512,512]{1,0:T(8,128)}, u32[]{:S(2)}) copy-start(f32[512,512]{1,0:T(8,128)} %c_ref.1) | copy-start | bytes 3145732
  1.9 1.2 %copy-start.1 = (f32[512,512]{1,0:T(8,128)S(1)}, f32[512,512]{1,0:T(8,128)}, u32[]{:S(2)}) copy-start(f32[512,512]{1,0:T(8,128)} %z_ref.1) | copy-start | bytes 3145732
  3.1 1.0 %copy-start.2 = (f32[512,256]{1,0:T(8,128)S(1)}, f32[512,256]{1,0:T(8,128)}, u32[]{:S(2)}) copy-start(f32[512,256]{1,0:T(8,128)} %h_ref.1) | copy-start | bytes 1572868

commit v4 on v3

--- a/solution.py
+++ b/solution.py
@@ -11,17 +11,20 @@
 MESH = pl.DeviceIdType.MESH
 NN = (((1,), (0,)), ((), ()))
 NT = (((1,), (1,)), ((), ()))
+TF = '01235678'
+XF = 1
 SP = 0
 REL = 1
 DIR = 1
-TP = '01235678'
+TP = '01235679'
 MP = '2345789a'
 HS = '1'
-HQ = '5'
-HF = '6'
+HQ = '6'
+HF = '7'
 HG = 'a'
 S = 32
 PIECE = 64
+XO = (2, 1, 3) if XF else (1, 3, 2)
 T = 16
 G = 128
 
@@ -146,6 +149,9 @@
     def mirror_out(i):
         part = pl.ds(i * PIECE, PIECE)
         put_if(near, c_ref.at[part], m.at[part], m_sem.at[i], c, r)
+
+    def mirror_far(i):
+        part = pl.ds(i * PIECE, PIECE)
         put_if(far, c_ref.at[part], relay.at[part], y_sem.at[i], c, x * 4 + r % 4)
 
     def mirror_pass(i):
@@ -192,6 +198,9 @@
         for i in range(8):
             if TP[i] == name:
                 mirror_out(i)
+        for i in range(8):
+            if TF[i] == name:
+                mirror_far(i)
         for i in range(8):
             if MP[i] == name:
                 mirror_pass(i)
@@ -271,14 +280,14 @@
         own = rt.at[h, share(c)]
         for j in range(1, 4):
             put(own, own, ag_sem.at[h, 0, j], r, x * 4 + (zh + j) % 4)
-        for d in (1, 3, 2):
+        for d in XO:
             put(own, own, ag_sem.at[h, d, 0], r, ((x + d) % 4) * 4 + zh)
 
     def spread_x(h):
         for j in range(1, 4):
             here = rt.at[h, share(x * 4 + (zh - j + 4) % 4)]
             got(here, ag_sem.at[h, 0, j])
-            for d in (1, 3, 2):
+            for d in XO:
                 put(here, here, ag_sem.at[h, d, j], r, ((x + d) % 4) * 4 + zh)
 
     products(0)

time: 94.5 us -> 93.3 us (0.987); the launches traced: 94.3 us -> 91.9 us
  Pallas kernels: 88.4 us -> 86.1 us
    pallas_call x1, Pallas kernels: 88.4 us -> 86.1 us  [per_device(): pl.pallas_call(kernel, out_shape=(jax.ShapeDtypeStruct((n, n), F32), jax....]
where the time goes in v4:
time: 93.3 us; the launch traced here: 91.9 us
  Pallas kernels  86.1 us (92%)
  local copies, waits for them, and re-layouts  5.19 us (6%)
    pallas_call x1, Pallas kernels, per_device(): pl.pallas_call(kernel, out_shape=(jax.ShapeDtypeStruct((n, n), F32), jax....  86.1 us
    unnamed x7, local copies, waits for them, and re-layouts  4.45 us

profile of v4, /device:TPU:5, one launch (start us, length us, event | category | flops | bytes accessed | tf_op | source)
XLA Modules:
  0.0 91.9 jit_solution(1369194592815183683)
XLA Ops:
  0.6 0.0 copy-start
  0.6 1.2 %copy-done = f32[512,512]{1,0:T(8,128)S(1)} copy-done((f32[512,512]{1,0:T(8,128)S(1)}, f32[512,512]{1,0:T(8,128)}, u32[]{:S(2)}) %copy-start) | copy-done | bytes 1048600
  1.9 0.0 copy-start.1
  1.9 1.2 %copy-done.1 = f32[512,512]{1,0:T(8,128)S(1)} copy-done((f32[512,512]{1,0:T(8,128)S(1)}, f32[512,512]{1,0:T(8,128)}, u32[]{:S(2)}) %copy-start.1) | copy-done | bytes 1048600
  3.1 0.0 copy-start.2
  3.1 1.0 %copy-done.2 = f32[512,256]{1,0:T(8,128)S(1)} copy-done((f32[512,256]{1,0:T(8,128)S(1)}, f32[512,256]{1,0:T(8,128)}, u32[]{:S(2)}) %copy-start.2) | copy-done | bytes 524312
  4.1 86.1 %shard_map.50 = (f32[512,512]{1,0:T(8,128)S(1)}, f32[512,32]{1,0:T(8,128)S(1)}) custom-call(f32[512,512]{1,0:T(8,128)S(1)} %copy-done, f32[512,512]{1,0:T(8,128)S(1)} %copy-done.1, f32[512,256]{1,0:T(8,128)S(1)} %copy-done.2), custom_call_target="tpu_custom_call" | custom-call | tf_op jit(solution)/shard_map/pallas_call | solution.py:392
  90.2 0.7 copy.5
  91.0 1.0 %copy.7 = f32[512,512]{1,0:T(8,128)} copy(f32[512,512]{1,0:T(8,128)S(1)} %get-tuple-element.6) | data formatting | bytes 2097152
Async XLA Ops:
  0.6 1.2 %copy-start = (f32[512,512]{1,0:T(8,128)S(1)}, f32[512,512]{1,0:T(8,128)}, u32[]{:S(2)}) copy-start(f32[512,512]{1,0:T(8,128)} %c_ref.1) | copy-start | bytes 3145732
  1.9 1.2 %copy-start.1 = (f32[512,512]{1,0:T(8,128)S(1)}, f32[512,512]{1,0:T(8,128)}, u32[]{:S(2)}) copy-start(f32[512,512]{1,0:T(8,128)} %z_ref.1) | copy-start | bytes 3145732
  3.1 1.0 %copy-start.2 = (f32[512,256]{1,0:T(8,128)S(1)}, f32[512,256]{1,0:T(8,128)}, u32[]{:S(2)}) copy-start(f32[512,256]{1,0:T(8,128)} %h_ref.1) | copy-start | bytes 1572868

commit v5 on v4

--- a/solution.py
+++ b/solution.py
@@ -21,7 +21,7 @@
 HS = '1'
 HQ = '6'
 HF = '7'
-HG = 'a'
+HG = 'b'
 S = 32
 PIECE = 64
 XO = (2, 1, 3) if XF else (1, 3, 2)

time: 93.3 us -> 93.3 us (level)
  no operation moved by 1% of the time
where the time goes in v5:
time: 93.3 us; the launch traced here: 91.9 us
  Pallas kernels  86.1 us (92%)
  local copies, waits for them, and re-layouts  5.19 us (6%)
    pallas_call x1, Pallas kernels, per_device(): pl.pallas_call(kernel, out_shape=(jax.ShapeDtypeStruct((n, n), F32), jax....  86.1 us
    unnamed x7, local copies, waits for them, and re-layouts  4.45 us

profile of v5, /device:TPU:5, one launch (start us, length us, event | category | flops | bytes accessed | tf_op | source)
XLA Modules:
  0.0 91.9 jit_solution(14427616279705861243)
XLA Ops:
  0.6 0.0 copy-start
  0.6 1.2 %copy-done = f32[512,512]{1,0:T(8,128)S(1)} copy-done((f32[512,512]{1,0:T(8,128)S(1)}, f32[512,512]{1,0:T(8,128)}, u32[]{:S(2)}) %copy-start) | copy-done | bytes 1048600
  1.9 0.0 copy-start.1
  1.9 1.2 %copy-done.1 = f32[512,512]{1,0:T(8,128)S(1)} copy-done((f32[512,512]{1,0:T(8,128)S(1)}, f32[512,512]{1,0:T(8,128)}, u32[]{:S(2)}) %copy-start.1) | copy-done | bytes 1048600
  3.1 0.0 copy-start.2
  3.1 1.0 %copy-done.2 = f32[512,256]{1,0:T(8,128)S(1)} copy-done((f32[512,256]{1,0:T(8,128)S(1)}, f32[512,256]{1,0:T(8,128)}, u32[]{:S(2)}) %copy-start.2) | copy-done | bytes 524312
  4.1 86.1 %shard_map.50 = (f32[512,512]{1,0:T(8,128)S(1)}, f32[512,32]{1,0:T(8,128)S(1)}) custom-call(f32[512,512]{1,0:T(8,128)S(1)} %copy-done, f32[512,512]{1,0:T(8,128)S(1)} %copy-done.1, f32[512,256]{1,0:T(8,128)S(1)} %copy-done.2), custom_call_target="tpu_custom_call" | custom-call | tf_op jit(solution)/shard_map/pallas_call | solution.py:392
  90.2 0.7 copy.5
  91.0 1.0 %copy.7 = f32[512,512]{1,0:T(8,128)} copy(f32[512,512]{1,0:T(8,128)S(1)} %get-tuple-element.6) | data formatting | bytes 2097152
Async XLA Ops:
  0.6 1.2 %copy-start = (f32[512,512]{1,0:T(8,128)S(1)}, f32[512,512]{1,0:T(8,128)}, u32[]{:S(2)}) copy-start(f32[512,512]{1,0:T(8,128)} %c_ref.1) | copy-start | bytes 3145732
  1.9 1.2 %copy-start.1 = (f32[512,512]{1,0:T(8,128)S(1)}, f32[512,512]{1,0:T(8,128)}, u32[]{:S(2)}) copy-start(f32[512,512]{1,0:T(8,128)} %z_ref.1) | copy-start | bytes 3145732
  3.1 1.0 %copy-start.2 = (f32[512,256]{1,0:T(8,128)S(1)}, f32[512,256]{1,0:T(8,128)}, u32[]{:S(2)}) copy-start(f32[512,256]{1,0:T(8,128)} %h_ref.1) | copy-start | bytes 1572868
